TPU v7x, 256 devices: a whole 4x4x8 slice. The times are simulated.
256 devices in a mesh: angle: 16 (over z, core), tile: 4 (over x), cuts: 4 (over y).
Axes of the slice: x: 4, y: 4, z: 8, core: 2. Of those that a mesh axis runs over, the one named last changes fastest.
Arguments:
- objects: float32 [16, 2, 512, 512], P('angle', None, ('tile', 'cuts')), may hold values from -6 to 6
- illumination: float32 [2, 128, 128], replicated, may hold values from -6 to 6
- positions: int32 [16, 256, 2], P('angle', ('tile', 'cuts')), may hold values from 0 to 384
- amplitudes: bfloat16 [16, 256, 128, 128], P('angle', ('tile', 'cuts')), may hold values from 0.25 to 2.5
- projector: bfloat16 [8192, 32768], P(None, ('angle', 'cuts')), may hold values from -0.0625 to 0.0625
Outputs:
- new_objects: float32 [16, 2, 512, 512], P('angle', None, ('tile', 'cuts'))
- volume: float32 [512, 32768], P('tile', ('angle', 'cuts'))
All inputs are finite; a program needn't handle non-finite values.
Results may differ from a plain program's by a relative error of at most 0.02.
Values may be sent and summed in bfloat16 or wider, within the bound.
A program may use at most 64 MiB of HBM per device.

v0:
```python
import jax
import jax.numpy as jnp
from jax import lax
from jax.sharding import PartitionSpec as P

step_size = 0.1


def dft_tables(patch_width):
    grid_index = jnp.arange(patch_width, dtype=jnp.int32)
    product_mod = grid_index[:, None] * grid_index[None, :] % patch_width
    phase_table = product_mod.astype(jnp.float32) * (2.0 * jnp.pi / patch_width)
    norm_scale = 1.0 / jnp.sqrt(jnp.float32(patch_width))
    table_real = (jnp.cos(phase_table) * norm_scale).astype(jnp.bfloat16)
    table_imag = (-jnp.sin(phase_table) * norm_scale).astype(jnp.bfloat16)
    table_wide = jnp.concatenate([table_real, table_imag], axis=1)
    table_tall = jnp.concatenate([table_real, table_imag], axis=0)
    return (table_wide, table_tall)


def right_product(stacked, table_wide, conjugate):
    edge_width = stacked.shape[-1]
    result = jnp.einsum("ncij,jk->ncik", stacked, table_wide, preferred_element_type=jnp.float32)
    from_real = result[:, 0]
    from_imag = result[:, 1]
    if conjugate:
        real_part = from_real[..., :edge_width] + from_imag[..., edge_width:]
        imag_part = from_imag[..., :edge_width] - from_real[..., edge_width:]
    else:
        real_part = from_real[..., :edge_width] - from_imag[..., edge_width:]
        imag_part = from_imag[..., :edge_width] + from_real[..., edge_width:]
    return jnp.stack([real_part, imag_part], axis=1)


def left_product(table_tall, stacked, conjugate):
    edge_width = stacked.shape[-1]
    result = jnp.einsum("kj,ncjm->nckm", table_tall, stacked, preferred_element_type=jnp.float32)
    from_real = result[:, 0]
    from_imag = result[:, 1]
    if conjugate:
        real_part = from_real[:, :edge_width, :] + from_imag[:, edge_width:, :]
        imag_part = from_imag[:, :edge_width, :] - from_real[:, edge_width:, :]
    else:
        real_part = from_real[:, :edge_width, :] - from_imag[:, edge_width:, :]
        imag_part = from_imag[:, :edge_width, :] + from_real[:, edge_width:, :]
    return jnp.stack([real_part, imag_part], axis=1)


def patch_update(object_half, illumination, place_list, amp_block, table_wide, table_tall):
    edge_width = illumination.shape[-1]
    zero_index = jnp.zeros((), jnp.int32)

    def cut_window(row_at, col_at):
        return lax.dynamic_slice(
            object_half, (zero_index, row_at, col_at), (2, edge_width, edge_width)
        )

    windows = jax.vmap(cut_window)(place_list[:, 0], place_list[:, 1]).astype(jnp.float32)
    probe_real = illumination[0]
    probe_imag = illumination[1]
    exit_real = probe_real * windows[:, 0] - probe_imag * windows[:, 1]
    exit_imag = probe_real * windows[:, 1] + probe_imag * windows[:, 0]
    exit_half = jnp.stack([exit_real, exit_imag], axis=1).astype(jnp.bfloat16)
    spread = right_product(exit_half, table_wide, False).astype(jnp.bfloat16)
    spectrum = left_product(table_tall, spread, False)
    modulus = jnp.sqrt(spectrum[:, 0] * spectrum[:, 0] + spectrum[:, 1] * spectrum[:, 1])
    scaling = amp_block.astype(jnp.float32) / jnp.maximum(modulus, 1.0)
    projected = (spectrum * scaling[:, None]).astype(jnp.bfloat16)
    back_half = right_product(projected, table_wide, True).astype(jnp.bfloat16)
    revised = left_product(table_tall, back_half, True)
    diff_real = revised[:, 0] - exit_real
    diff_imag = revised[:, 1] - exit_imag
    update_real = step_size * (probe_real * diff_real + probe_imag * diff_imag)
    update_imag = step_size * (probe_real * diff_imag - probe_imag * diff_real)
    patch_terms = jnp.stack([update_real, update_imag], axis=1)
    canvas = jnp.zeros(object_half.shape, jnp.float32)

    def place_one(counter, canvas_now):
        row_at = place_list[counter, 0]
        col_at = place_list[counter, 1]
        current = lax.dynamic_slice(
            canvas_now, (zero_index, row_at, col_at), (2, edge_width, edge_width)
        )
        return lax.dynamic_update_slice(
            canvas_now, current + patch_terms[counter], (zero_index, row_at, col_at)
        )

    return lax.fori_loop(0, place_list.shape[0], place_one, canvas)


def body(objects, illumination, positions, amplitudes, projector):
    tile_count = lax.axis_size("tile")
    cuts_count = lax.axis_size("cuts")
    angle_count = lax.axis_size("angle")
    ang_dev = objects.shape[0]
    band_rows = objects.shape[2]
    image_width = objects.shape[3]
    edge_width = illumination.shape[-1]
    voxel_count = projector.shape[1]
    table_wide, table_tall = dft_tables(edge_width)
    object_half = objects.astype(jnp.bfloat16)
    whole_half = lax.all_gather(object_half, ("tile", "cuts"), axis=2, tiled=True)
    partial_value = jnp.stack(
        [
            patch_update(
                whole_half[0], illumination, positions[0], amplitudes[0], table_wide, table_tall
            )
        ],
        axis=0,
    )
    weight_view = projector.reshape(angle_count, ang_dev, image_width, voxel_count)
    summed = lax.psum(partial_value.astype(jnp.bfloat16), ("tile", "cuts")).astype(jnp.float32)
    band_start = (lax.axis_index("tile") * cuts_count + lax.axis_index("cuts")) * band_rows
    new_objects = objects + lax.dynamic_slice_in_dim(summed, band_start, band_rows, 2)
    slab_rows = image_width // tile_count
    slab_start = lax.axis_index("tile") * slab_rows
    imag_slab = lax.dynamic_slice_in_dim(whole_half[:, 1], slab_start, slab_rows, 1).astype(
        jnp.float32
    ) + lax.dynamic_slice_in_dim(summed[:, 1], slab_start, slab_rows, 1)
    phase_slab = imag_slab.astype(jnp.bfloat16)
    gathered = lax.all_gather(phase_slab[None], "angle", axis=0, tiled=True)
    volume = jnp.einsum("adyu,aduv->yv", gathered, weight_view, preferred_element_type=jnp.float32)
    return (new_objects, volume)


def solution(mesh):
    in_specs = (
        P("angle", None, ("tile", "cuts"), None),
        P(),
        P("angle", ("tile", "cuts"), None),
        P("angle", ("tile", "cuts"), None, None),
        P(None, ("angle", "cuts")),
    )
    out_specs = (P("angle", None, ("tile", "cuts"), None), P("tile", ("angle", "cuts")))
    return jax.shard_map(body, mesh=mesh, in_specs=in_specs, out_specs=out_specs, check_vma=False)
```

profile of v0, /device:TPU:1, one launch (start us, length us, event | category | flops | bytes accessed | tf_op | source)
XLA Modules:
  0.0 393.0 jit_solution(9680044881272197370)
XLA Ops:
  12.1 49.1 %all-gather.3.cloned.1.call-done = bf16[1,2,512,512]{3,2,1,0:T(8,128)(2,1)} async-done(((bf16[1,2,32,512]{3,2,1,0:T(8,128)(2,1)}), bf16[1,2,512,512]{3,2,1,0:T(8,128)(2,1)}) %all-gather.3.cloned.1.call-update) | async-done | bytes 1048592 | tf_op jit(solution)/shard_map/all_gather | solution.py:102
  61.2 46.0 %while.15 = (s32[]{:T(128)}, bf16[2,512,512]{2,1,0:T(8,128)(2,1)}, s32[16,3]{0,1:T(4,128)S(1)}, bf16[16,2,128,128]{3,2,0,1:T(8,128)(2,1)S(1)}, s32[]{:T(128)}) while((s32[]{:T(128)}, bf16[2,512,512]{2,1,0:T(8,128)(2,1)}, s32[16,3]{0,1:T(4,128)S(1)}, bf16[16,2,128,128]{3,2,0,1:T(8,128)(2,1)S(1)}, s32[]{:T(128)}) %tuple.77), condition=%wide.while_cond, body=%wide.while_body.sunk | while | flops 2 | bytes 131189 | solution.py:54
  64.7 2.3 bitcast_dynamic-update-slice_fusion.2
  67.5 2.3 bitcast_dynamic-update-slice_fusion.2
  70.4 2.3 bitcast_dynamic-update-slice_fusion.2
  73.3 2.3 bitcast_dynamic-update-slice_fusion.2
  79.0 2.3 bitcast_dynamic-update-slice_fusion.2
  81.9 2.3 bitcast_dynamic-update-slice_fusion.2
  84.8 2.3 bitcast_dynamic-update-slice_fusion.2
  87.7 2.3 bitcast_dynamic-update-slice_fusion.2
  90.5 2.3 bitcast_dynamic-update-slice_fusion.2
  93.4 2.3 bitcast_dynamic-update-slice_fusion.2
  96.3 2.3 bitcast_dynamic-update-slice_fusion.2
  99.2 2.3 bitcast_dynamic-update-slice_fusion.2
  104.9 2.3 bitcast_dynamic-update-slice_fusion.2
  116.8 121.8 %while.14 = (s32[]{:T(128)}, f32[2,512,512]{2,1,0:T(8,128)S(1)}, s32[16,2]{0,1:T(2,128)S(1)}, f32[16,2,128,128]{3,2,0,1:T(8,128)}, s32[]{:T(128)}, /*index=5*/s32[]{:T(128)}, s32[]{:T(128)}) while((s32[]{:T(128)}, f32[2,512,512]{2,1,0:T(8,128)S(1)}, s32[16,2]{0,1:T(2,128)S(1)}, f32[16,2,128,128]{3,2,0,1:T(8,128)}, s32[]{:T(128)}, ...), condition=%wide.region_1.2_spmd, body=%wide.region_0.1_spmd.sunk | while | flops 32776 | bytes 655541 | solution.py:88
  122.0 2.5 dynamic_update_slice.8
  129.7 2.5 dynamic_update_slice.8
  137.4 2.3 dynamic_update_slice.8
  152.3 2.5 dynamic_update_slice.8
  160.0 2.5 dynamic_update_slice.8
  167.7 2.5 dynamic_update_slice.8
  182.8 2.5 dynamic_update_slice.8
  197.9 2.5 dynamic_update_slice.8
  205.6 2.4 dynamic_update_slice.8
  213.2 2.4 dynamic_update_slice.8
  220.8 2.5 dynamic_update_slice.8
  228.5 2.5 dynamic_update_slice.8
  236.3 2.3 dynamic_update_slice.8
  240.2 96.9 %all-reduce.2.cloned.1.call-done = bf16[1,2,512,512]{3,2,1,0:T(8,128)(2,1)} async-done(((bf16[1,2,512,512]{3,2,1,0:T(8,128)(2,1)}), bf16[1,2,512,512]{3,2,1,0:T(8,128)(2,1)}) %all-reduce.2.cloned.1.call-update) | async-done | bytes 1048592 | tf_op jit(solution)/shard_map/psum | solution.py:112
  340.1 40.4 %all-gather.5.cloned.1.call-done = bf16[16,1,128,512]{3,2,1,0:T(8,128)(2,1)} async-done(((bf16[1,1,128,512]{3,2,1,0:T(8,128)(2,1)}), bf16[16,1,128,512]{3,2,1,0:T(8,128)(2,1)}) %all-gather.5.cloned.1.call-update) | async-done | bytes 2097168 | tf_op jit(solution)/shard_map/all_gather | solution.py:121
  380.5 6.0 %fusion.3 = f32[128,512]{1,0:T(8,128)} fusion(bf16[16,512,512]{2,1,0:T(8,128)(2,1)} %bitcast.136, bf16[16,1,128,512]{3,2,1,0:T(8,128)(2,1)} %all-gather.5.cloned.1.call-done), kind=kOutput, calls=%fused_computation.20 | convolution fusion | flops 1073741824 | bytes 10747904 | tf_op jit(solution)/shard_map/adyu,aduv->yv/dot_general | solution.py:122
  (116 shorter events, 67.5 us)
Async XLA Ops:
  7.2 54.0 %all-gather.3.cloned.1.call-start = ((), (), s32[]{:S(2)}) async-start(), calls=%async_computation | async-start | bytes 1114112 | tf_op jit(solution)/shard_map/all_gather | solution.py:102
  8.8 328.4 %all-reduce.2.cloned.1.call-start = ((), (), s32[]{:S(2)}) async-start(), calls=%async_computation.1 | async-start | bytes 2097152 | tf_op jit(solution)/shard_map/psum | solution.py:112
  116.1 0.7 copy-start.3
  238.6 1.6 copy-start.1
  239.8 140.7 %all-gather.5.cloned.1.call-start = ((), (), s32[]{:S(2)}) async-start(), calls=%async_computation.2 | async-start | bytes 2228224 | tf_op jit(solution)/shard_map/all_gather | solution.py:121
  337.2 2.0 copy-start
  338.4 1.0 copy-start.2
Sparse Core Ops, SparseCore 0:
  11.1 50.0 all-gather.2
  239.9 97.2 all-reduce.1
  339.6 40.8 all-gather.4
where the time goes:
time: 395 us; the launch traced here: 393 us
  waiting for transfers between devices  186 us (47%)
  local copies, waits for them, and re-layouts  99.6 us (25%)
  loops' own time  57.9 us (15%)
  other arithmetic  26.2 us (7%)
  between operations  14 us (4%)
  matrix products  8.83 us (2%)
    psum x1, waiting for transfers between devices, body(): lax.psum(partial_value.astype(jnp.bfloat16), ('tile', 'cuts'))  96.9 us
    another operation x1, loops' own time, patch_update(): return lax.fori_loop(0, place_list.shape[0], place_one, canvas)  57.7 us
    all_gather x1, waiting for transfers between devices, body(): lax.all_gather(object_half, ('tile', 'cuts'), axis=2, tiled=True)  49.1 us
    gather x48, local copies, waits for them, and re-layouts  45.8 us
    all_gather x1, waiting for transfers between devices, body(): gathered = lax.all_gather(phase_slab[None], 'angle', axis=0, tiled=True)  40.4 us
    dynamic_update_slice x16, local copies, waits for them, and re-layouts, place_one(): lax.dynamic_update_slice(canvas_now, current + patch_terms[counter], (zer...  38.4 us
    add x16, other arithmetic, place_one(): current + patch_terms[counter]  16.4 us
    dynamic_slice x16, local copies, waits for them, and re-layouts, place_one(): col_at = place_list[counter, 1]  9.38 us
  transfers between devices with their start and end apart: 3, of which 3 were waited for; matrix products, arithmetic and copies ran while one was open for 1% of the time, Pallas kernels for 0%

commit v1 on v0

v1 whole, which is shorter than its diff:
```python
import functools

import jax
import jax.numpy as jnp
import numpy as np
from jax import lax
from jax.experimental import pallas as pl
from jax.experimental.pallas import tpu as pltpu
from jax.sharding import PartitionSpec as P

MESH = pl.DeviceIdType.MESH
STEP_SIZE = 0.1
LANES = 128
CORES = 2


def dft_table(width):
    index = np.arange(width)
    phase = (index[:, None] * index[None, :] % width) * (2.0 * np.pi / width)
    scale = 1.0 / np.sqrt(width)
    table = np.concatenate([np.cos(phase) * scale, -np.sin(phase) * scale], axis=1)
    return jnp.asarray(table.astype(np.float32)).astype(jnp.bfloat16)


def plane_offsets(n_tile, n_cuts):
    pairs = [(dt, dc) for dt in range(n_tile) for dc in range(n_cuts) if (dt, dc) != (0, 0)]
    hops = lambda d, n: min(d, n - d)
    return sorted(pairs, key=lambda o: -(hops(o[0], n_tile) + hops(o[1], n_cuts)))


def gather_kernel(n_tile, n_cuts, obj_ref, img_ref, mine, landed, send_sem, recv_sem):
    t, c = lax.axis_index("tile"), lax.axis_index("cuts")
    rows = obj_ref.shape[1]
    offsets = plane_offsets(n_tile, n_cuts)

    def peer(dt, dc):
        return {"tile": lax.rem(t + dt, n_tile), "cuts": lax.rem(c + dc, n_cuts)}

    barrier = pltpu.get_barrier_semaphore()
    for dt, dc in offsets:
        pl.semaphore_signal(barrier, inc=1, device_id=peer(dt, dc), device_id_type=MESH)
    mine[...] = obj_ref[...].astype(jnp.bfloat16)
    pl.semaphore_wait(barrier, len(offsets))

    copies = []
    for i, (dt, dc) in enumerate(offsets):
        copy = pltpu.make_async_remote_copy(
            src_ref=mine,
            dst_ref=landed.at[i],
            send_sem=send_sem.at[i],
            recv_sem=recv_sem.at[i],
            device_id=peer(dt, dc),
            device_id_type=MESH,
        )
        copy.start()
        copies.append(copy)

    def unpack(block, band):
        at = pl.ds(pl.multiple_of(band * rows, rows), rows)
        for part in range(2):
            for j in range(img_ref.shape[1]):
                img_ref[part, j, at, :] = block[part, :, j * LANES : (j + 1) * LANES].astype(
                    jnp.float32
                )

    unpack(mine, t * n_cuts + c)
    for i in reversed(range(len(offsets))):
        dt, dc = offsets[i]
        copies[i].wait_recv()
        band = lax.rem(t + n_tile - dt, n_tile) * n_cuts + lax.rem(c + n_cuts - dc, n_cuts)
        unpack(landed.at[i], band)
    for copy in copies:
        copy.wait_send()


def patch_kernel(pos_ref, img_ref, amp_ref, probe_ref, table_ref, out_ref, canvas, fwd, bwd):
    width = probe_ref.shape[-1]
    strips = img_ref.shape[1]
    f_re, f_im = table_ref[:, :width], table_ref[:, width:]
    fwd[:width, :width] = f_re
    fwd[:width, width:] = f_im
    fwd[width:, :width] = -f_im
    fwd[width:, width:] = f_re
    bwd[:width, :width] = f_re
    bwd[:width, width:] = -f_im
    bwd[width:, :width] = f_im
    bwd[width:, width:] = f_re
    canvas[...] = jnp.zeros_like(canvas)
    lane = lax.broadcasted_iota(jnp.int32, (width, width), 1)

    def dot(a, b):
        return jnp.dot(a, b, preferred_element_type=jnp.float32)

    def quad(a, b, c, d):
        return jnp.concatenate(
            [jnp.concatenate([a, b], axis=1), jnp.concatenate([c, d], axis=1)], axis=0
        )

    def swap(x):
        w = width
        return quad(x[:w, :w], x[w:, :w], x[:w, w:], x[w:, w:])

    def pair(i, carry):
        exits = []
        for k in range(2):
            row, col = pos_ref[2 * i + k, 0], pos_ref[2 * i + k, 1]
            strip, shift = col // LANES, lax.rem(col, LANES)

            def window(part):
                left = img_ref[part, strip, pl.ds(row, width), :]
                right = img_ref[part, jnp.minimum(strip + 1, strips - 1), pl.ds(row, width), :]
                joined = jnp.where(lane >= shift, left, right)
                return pltpu.roll(joined, lax.rem(LANES - shift, LANES), 1)

            w_re, w_im = window(0), window(1)
            p_re, p_im = probe_ref[0], probe_ref[1]
            exits.append((p_re * w_re - p_im * w_im, p_re * w_im + p_im * w_re))
        ex = quad(*exits[0], *exits[1])
        spread = dot(ex.astype(jnp.bfloat16), fwd[...]).astype(jnp.bfloat16)
        spectrum = dot(bwd[...], swap(spread))
        s_re, s_im = spectrum[:width], spectrum[width:]
        amp = jnp.concatenate([amp_ref[2 * i], amp_ref[2 * i + 1]], axis=1).astype(jnp.float32)
        scaling = amp * lax.rsqrt(jnp.maximum(s_re * s_re + s_im * s_im, 1.0))
        projected = jnp.concatenate([s_re * scaling, s_im * scaling], axis=0)
        back = dot(swap(projected.astype(jnp.bfloat16)), bwd[...]).astype(jnp.bfloat16)
        revised = dot(fwd[...], swap(back))
        for k in range(2):
            row, col = pos_ref[2 * i + k, 0], pos_ref[2 * i + k, 1]
            strip, shift = col // LANES, lax.rem(col, LANES)
            cols = slice(k * width, (k + 1) * width)
            d_re = revised[:width, cols] - exits[k][0]
            d_im = revised[width:, cols] - exits[k][1]
            p_re, p_im = probe_ref[0], probe_ref[1]
            u_re = STEP_SIZE * (p_re * d_re + p_im * d_im)
            u_im = STEP_SIZE * (p_re * d_im - p_im * d_re)
            for part, term in ((0, u_re), (1, u_im)):
                turned = pltpu.roll(term, shift, 1)
                at = pl.ds(row, width)
                canvas[part, strip, at, :] += jnp.where(lane >= shift, turned, 0.0)
                canvas[part, strip + 1, at, :] += jnp.where(lane < shift, turned, 0.0)
        return carry

    lax.fori_loop(0, amp_ref.shape[0] // 2, pair, 0)
    for part in range(2):
        for j in range(strips):
            out_ref[part, :, j * LANES : (j + 1) * LANES] = canvas[part, j].astype(jnp.bfloat16)


def finish_kernel(
    n_angle,
    n_tile,
    n_cuts,
    obj_ref,
    part_ref,
    proj_hbm,
    new_ref,
    vol_ref,
    proj,
    landed,
    phase,
    proj_sem,
    sum_send,
    sum_recv,
    z_send,
    z_recv,
    y_send,
    y_recv,
    s_send,
    s_recv,
):
    a, t, c = lax.axis_index("angle"), lax.axis_index("tile"), lax.axis_index("cuts")
    z, core = a // CORES, lax.rem(a, CORES)
    n_z = n_angle // CORES
    rows, pixels = obj_ref.shape[1:]
    offsets = plane_offsets(n_tile, n_cuts)
    z_steps = sorted(range(1, n_z), key=lambda d: min(d, n_z - d))
    y_steps = list(range(1, n_cuts))

    def plane_peer(dt, dc):
        return {"tile": lax.rem(t + dt, n_tile), "cuts": lax.rem(c + dc, n_cuts)}

    def z_peer(dz):
        return {"angle": lax.rem(z + dz, n_z) * CORES + core}

    def y_peer(dc):
        return {"cuts": lax.rem(c + dc, n_cuts)}

    sibling = {"angle": z * CORES + (1 - core)}

    projector_copy = pltpu.make_async_copy(proj_hbm, proj, proj_sem)
    projector_copy.start()

    barrier = pltpu.get_barrier_semaphore()
    greeted = [plane_peer(*o) for o in offsets] + [z_peer(d) for d in z_steps] + [sibling]
    for device in greeted:
        pl.semaphore_signal(barrier, inc=1, device_id=device, device_id_type=MESH)
    pl.semaphore_wait(barrier, len(greeted))

    def remote(src, dst, send_sem, recv_sem, device):
        copy = pltpu.make_async_remote_copy(
            src_ref=src,
            dst_ref=dst,
            send_sem=send_sem,
            recv_sem=recv_sem,
            device_id=device,
            device_id_type=MESH,
        )
        copy.start()
        return copy

    def band_at(band):
        return pl.ds(pl.multiple_of(band * rows, rows), rows)

    sums = {}
    for part in (1, 0):
        for i, (dt, dc) in enumerate(offsets):
            band = lax.rem(t + dt, n_tile) * n_cuts + lax.rem(c + dc, n_cuts)
            sums[part, i] = remote(
                part_ref.at[part, band_at(band), :],
                landed.at[part, i],
                sum_send.at[part, i],
                sum_recv.at[part, i],
                plane_peer(dt, dc),
            )

    def summed(part):
        total = part_ref[part, band_at(t * n_cuts + c), :].astype(jnp.float32)
        for i in range(len(offsets)):
            sums[part, i].wait_recv()
        for i in range(len(offsets)):
            total = total + landed[part, i].astype(jnp.float32)
        return total

    update = summed(1)
    half = obj_ref[1].astype(jnp.bfloat16).astype(jnp.float32)
    phase[a, c] = (half + update).astype(jnp.bfloat16)
    new_ref[1] = obj_ref[1] + update

    sent = []
    z_copies, y_copies, s_copies = {}, {}, {}

    def source(dz, dc):
        return phase.at[lax.rem(z + n_z - dz, n_z) * CORES + core, lax.rem(c + n_cuts - dc, n_cuts)]

    def to_sibling(dz, dc):
        block = source(dz, dc)
        s_copies[dz, dc] = remote(block, block, s_send.at[dz, dc], s_recv.at[dz, dc], sibling)

    def to_cuts(dz):
        block = source(dz, 0)
        for dc in y_steps:
            y_copies[dz, dc] = remote(block, block, y_send.at[dz, dc], y_recv.at[dz, dc], y_peer(dc))

    own = source(0, 0)
    for dz in z_steps:
        z_copies[dz] = remote(own, own, z_send.at[dz], z_recv.at[dz], z_peer(dz))
    to_cuts(0)
    to_sibling(0, 0)
    for dz in z_steps:
        z_copies[dz].wait_recv()
        to_cuts(dz)
        to_sibling(dz, 0)

    update = summed(0)
    new_ref[0] = obj_ref[0] + update

    projector_copy.wait()

    def project(angle, first):
        block = phase[angle].reshape(n_cuts * rows, pixels)
        weights = proj[pl.ds(pl.multiple_of(angle * pixels, pixels), pixels), :]
        term = jnp.dot(block, weights, preferred_element_type=jnp.float32)
        if first:
            vol_ref[...] = term
        else:
            vol_ref[...] += term

    order = [0] + z_steps
    for dz in order:
        for dc in y_steps:
            y_copies[dz, dc].wait_recv()
            to_sibling(dz, dc)
        project(lax.rem(z + n_z - dz, n_z) * CORES + core, dz == 0)
    for dz in order:
        for dc in [0] + y_steps:
            s_copies[dz, dc].wait_recv()
        project(lax.rem(z + n_z - dz, n_z) * CORES + (1 - core), False)

    for group in (sums, z_copies, y_copies, s_copies):
        for copy in group.values():
            copy.wait_send()


def body(objects, illumination, positions, amplitudes, projector):
    n_angle, n_tile, n_cuts = (lax.axis_size(n) for n in ("angle", "tile", "cuts"))
    _, _, rows, pixels = objects.shape
    width = illumination.shape[-1]
    strips = pixels // LANES
    n_peers = n_tile * n_cuts - 1
    vmem = pl.BlockSpec(memory_space=pltpu.VMEM)
    obj = objects[0]

    image = pl.pallas_call(
        functools.partial(gather_kernel, n_tile, n_cuts),
        out_shape=jax.ShapeDtypeStruct((2, strips, pixels, LANES), jnp.float32),
        in_specs=[vmem],
        out_specs=vmem,
        scratch_shapes=[
            pltpu.VMEM((2, rows, pixels), jnp.bfloat16),
            pltpu.VMEM((n_peers, 2, rows, pixels), jnp.bfloat16),
            pltpu.SemaphoreType.DMA((n_peers,)),
            pltpu.SemaphoreType.DMA((n_peers,)),
        ],
        compiler_params=pltpu.CompilerParams(
            collective_id=0, has_side_effects=True, vmem_limit_bytes=32 * 2**20
        ),
        name="gather_image",
    )(obj)

    partial_sum = pl.pallas_call(
        patch_kernel,
        out_shape=jax.ShapeDtypeStruct((2, pixels, pixels), jnp.bfloat16),
        in_specs=[pl.BlockSpec(memory_space=pltpu.SMEM), vmem, vmem, vmem, vmem],
        out_specs=vmem,
        scratch_shapes=[
            pltpu.VMEM((2, strips + 1, pixels, LANES), jnp.float32),
            pltpu.VMEM((2 * width, 2 * width), jnp.bfloat16),
            pltpu.VMEM((2 * width, 2 * width), jnp.bfloat16),
        ],
        compiler_params=pltpu.CompilerParams(vmem_limit_bytes=32 * 2**20),
        name="patch_update",
    )(positions[0], image, amplitudes[0], illumination, dft_table(width))

    n_z = n_angle // CORES
    new_objects, volume = pl.pallas_call(
        functools.partial(finish_kernel, n_angle, n_tile, n_cuts),
        out_shape=(
            jax.ShapeDtypeStruct((2, rows, pixels), jnp.float32),
            jax.ShapeDtypeStruct((n_cuts * rows, projector.shape[1]), jnp.float32),
        ),
        in_specs=[vmem, vmem, pl.BlockSpec(memory_space=pl.ANY)],
        out_specs=(vmem, vmem),
        scratch_shapes=[
            pltpu.VMEM(projector.shape, jnp.bfloat16),
            pltpu.VMEM((2, n_peers, rows, pixels), jnp.bfloat16),
            pltpu.VMEM((n_angle, n_cuts, rows, pixels), jnp.bfloat16),
            pltpu.SemaphoreType.DMA,
            pltpu.SemaphoreType.DMA((2, n_peers)),
            pltpu.SemaphoreType.DMA((2, n_peers)),
            pltpu.SemaphoreType.DMA((n_z,)),
            pltpu.SemaphoreType.DMA((n_z,)),
            pltpu.SemaphoreType.DMA((n_z, n_cuts)),
            pltpu.SemaphoreType.DMA((n_z, n_cuts)),
            pltpu.SemaphoreType.DMA((n_z, n_cuts)),
            pltpu.SemaphoreType.DMA((n_z, n_cuts)),
        ],
        compiler_params=pltpu.CompilerParams(
            collective_id=1, has_side_effects=True, vmem_limit_bytes=32 * 2**20
        ),
        name="sum_and_project",
    )(obj, partial_sum, projector)
    return new_objects[None], volume


def solution(mesh):
    in_specs = (
        P("angle", None, ("tile", "cuts"), None),
        P(),
        P("angle", ("tile", "cuts"), None),
        P("angle", ("tile", "cuts"), None, None),
        P(None, ("angle", "cuts")),
    )
    out_specs = (P("angle", None, ("tile", "cuts"), None), P("tile", ("angle", "cuts")))
    return jax.shard_map(body, mesh=mesh, in_specs=in_specs, out_specs=out_specs, check_vma=False)
```

time: 395 us -> 74.6 us (0.19)
  waiting for transfers between devices: 186 us -> 0 us
  local copies, waits for them, and re-layouts: 99.6 us -> 9.18 us
  Pallas kernels: 0 us -> 64.5 us
  loops' own time: 57.9 us -> 0 us
  other arithmetic: 26.2 us -> 0 us
  between operations: 14 us -> 0.67 us
  matrix products: 8.83 us -> 0 us
    psum x1 -> x0, waiting for transfers between devices: 96.9 us -> none  [body(): lax.psum(partial_value.astype(jnp.bfloat16), ('tile', 'cuts'))]
    all_gather x2 -> x0, waiting for transfers between devices: 89.4 us -> none  [the longest x1 49.1 us: body(): lax.all_gather(object_half, ('tile', 'cuts'), axis=2, tiled=True)]
    pallas_call x0 -> x3, Pallas kernels: none -> 64.5 us  [the longest x1 36.1 us: body(): pl.pallas_call(functools.partial(finish_kernel, n_angle, n_tile, n_cuts),...]
    another operation x2 -> x0, loops' own time: 57.9 us -> none  [the longest x1 57.7 us: patch_update(): return lax.fori_loop(0, place_list.shape[0], place_one, canvas)]
    gather x48 -> x0, local copies, waits for them, and re-layouts: 45.8 us -> none
    dynamic_update_slice x16 -> x0, local copies, waits for them, and re-layouts: 38.4 us -> none  [place_one(): lax.dynamic_update_slice(canvas_now, current + patch_terms[counter], (zer...]
    add x17 -> x0, other arithmetic: 17 us -> none  [the longest x16 16.4 us: place_one(): current + patch_terms[counter]]
    dynamic_slice x16 -> x0, local copies, waits for them, and re-layouts: 9.38 us -> none  [place_one(): col_at = place_list[counter, 1]]
  transfers between devices with their start and end apart: 3 -> 0, of which waited for: 3 -> 0; matrix products, arithmetic and copies ran while one was open for 1% -> 0% of each run, Pallas kernels for 0% -> 0%
where the time goes in v1:
time: 74.6 us; the launch traced here: 74.3 us
  Pallas kernels  64.5 us (86%)
  local copies, waits for them, and re-layouts  9.18 us (12%)
    pallas_call x1, Pallas kernels, body(): pl.pallas_call(functools.partial(finish_kernel, n_angle, n_tile, n_cuts),...  36.1 us
    pallas_call x1, Pallas kernels, body(): pl.pallas_call(functools.partial(gather_kernel, n_tile, n_cuts), out_shap...  19.6 us
    pallas_call x1, Pallas kernels, body(): pl.pallas_call(patch_kernel, out_shape=jax.ShapeDtypeStruct((2, pixels, p...  8.77 us
    unnamed x12, local copies, waits for them, and re-layouts  8.42 us

profile of v1, /device:TPU:1, one launch (start us, length us, event | category | flops | bytes accessed | tf_op | source)
XLA Modules:
  0.0 74.3 jit_solution(14517317917613936931)
XLA Ops:
  0.6 0.8 %copy.8.pos_ref = s32[16,2]{1,0:T(8,128)S(1)} copy(s32[16,2]{0,1:T(2,128)} %bitcast.8) | data formatting | bytes 256 | tf_op jit(solution)/shard_map/squeeze | solution.py:332
  1.4 0.0 copy-start.1
  1.4 0.9 %copy-done.1 = f32[1,2,32,512]{3,2,1,0:T(8,128)S(1)} copy-done((f32[1,2,32,512]{3,2,1,0:T(8,128)S(1)}, f32[1,2,32,512]{3,2,1,0:T(8,128)}, u32[]{:S(2)}) %copy-start.1) | copy-done | bytes 131096
  2.3 19.6 %gather_image.1.img_ref = f32[2,4,512,128]{3,2,1,0:T(8,128)S(1)} custom-call(f32[2,32,512]{2,1,0:T(8,128)S(1)} %bitcast.4), custom_call_target="tpu_custom_call" | custom-call | tf_op jit(solution)/shard_map/gather_image/pallas_call | solution.py:303
  21.9 0.0 copy-start.2
  21.9 1.0 %copy-done.2 = bf16[1,16,128,128]{3,2,1,0:T(8,128)(2,1)S(1)} copy-done((bf16[1,16,128,128]{3,2,1,0:T(8,128)(2,1)S(1)}, bf16[1,16,128,128]{3,2,1,0:T(8,128)(2,1)}, u32[]{:S(2)}) %copy-start.2) | copy-done | bytes 524312
  22.9 0.0 copy-start.3
  22.9 0.9 %copy-done.3 = f32[2,128,128]{2,1,0:T(8,128)S(1)} copy-done((f32[2,128,128]{2,1,0:T(8,128)S(1)}, f32[2,128,128]{2,1,0:T(8,128)}, u32[]{:S(2)}) %copy-start.3) | copy-done | bytes 131096
  23.8 0.0 copy-start.4
  23.8 0.8 %copy-done.4 = bf16[128,256]{1,0:T(8,128)(2,1)S(1)} copy-done((bf16[128,256]{1,0:T(8,128)(2,1)S(1)}, bf16[128,256]{1,0:T(8,128)(2,1)}, u32[]{:S(2)}) %copy-start.4) | copy-done | bytes 65560
  24.7 8.8 %patch_update.1.part_ref = bf16[2,512,512]{2,1,0:T(8,128)(2,1)S(1)} custom-call(s32[16,2]{1,0:T(8,128)S(1)} %copy.8.pos_ref, f32[2,4,512,128]{3,2,1,0:T(8,128)S(1)} %gather_image.1.img_ref, bf16[16,128,128]{2,1,0:T(8,128)(2,1)S(1)} %bitcast.6, f32[2,128,128]{2,1,0:T(8,128)S(1)} %copy-done.3, bf16[128,256]{1,0:T(8,128)(2,1)S(1)} %copy-done.4), custom_call_target="tpu_custom_call" | custom-call | tf_op jit(solution)/shard_map/patch_update/pallas_call | solution.py:320
  33.5 0.0 copy-start
  33.5 3.4 %copy-done = bf16[8192,512]{1,0:T(8,128)(2,1)S(1)} copy-done((bf16[8192,512]{1,0:T(8,128)(2,1)S(1)}, bf16[8192,512]{1,0:T(8,128)(2,1)}, u32[]{:S(2)}) %copy-start) | copy-done | bytes 8388632
  36.9 36.1 %sum_and_project.1 = (f32[2,32,512]{2,1,0:T(8,128)S(1)}, f32[128,512]{1,0:T(8,128)S(1)}) custom-call(f32[2,32,512]{2,1,0:T(8,128)S(1)} %bitcast.5, bf16[2,512,512]{2,1,0:T(8,128)(2,1)S(1)} %patch_update.1.part_ref, bf16[8192,512]{1,0:T(8,128)(2,1)S(1)} %copy-done), custom_call_target="tpu_custom_call" | custom-call | tf_op jit(solution)/shard_map/sum_and_project/pallas_call | solution.py:335
  73.0 0.7 copy.11
  73.6 0.7 copy.12
Async XLA Ops:
  1.4 0.9 %copy-start.1 = (f32[1,2,32,512]{3,2,1,0:T(8,128)S(1)}, f32[1,2,32,512]{3,2,1,0:T(8,128)}, u32[]{:S(2)}) copy-start(f32[1,2,32,512]{3,2,1,0:T(8,128)} %param.6) | copy-start | bytes 393220
  21.9 1.0 %copy-start.2 = (bf16[1,16,128,128]{3,2,1,0:T(8,128)(2,1)S(1)}, bf16[1,16,128,128]{3,2,1,0:T(8,128)(2,1)}, u32[]{:S(2)}) copy-start(bf16[1,16,128,128]{3,2,1,0:T(8,128)(2,1)} %param.9) | copy-start | bytes 1572868
  22.9 0.9 %copy-start.3 = (f32[2,128,128]{2,1,0:T(8,128)S(1)}, f32[2,128,128]{2,1,0:T(8,128)}, u32[]{:S(2)}) copy-start(f32[2,128,128]{2,1,0:T(8,128)} %probe_ref.1) | copy-start | bytes 393220
  23.8 0.8 %copy-start.4 = (bf16[128,256]{1,0:T(8,128)(2,1)S(1)}, bf16[128,256]{1,0:T(8,128)(2,1)}, u32[]{:S(2)}) copy-start(bf16[128,256]{1,0:T(8,128)(2,1)} %constant.6.table_ref) | copy-start | bytes 196612
  33.5 3.4 %copy-start = (bf16[8192,512]{1,0:T(8,128)(2,1)S(1)}, bf16[8192,512]{1,0:T(8,128)(2,1)}, u32[]{:S(2)}) copy-start(bf16[8192,512]{1,0:T(8,128)(2,1)} %proj_hbm.1) | copy-start | bytes 25165828

commit v2 on v0

v2 whole, which is shorter than its diff:
```python
import functools

import jax
import jax.numpy as jnp
import numpy as np
from jax import lax
from jax.experimental import pallas as pl
from jax.experimental.pallas import tpu as pltpu
from jax.sharding import PartitionSpec as P

MESH = pl.DeviceIdType.MESH
STEP_SIZE = 0.1
LANES = 128
CORES = 2
COPIES = 160
F32, BF16 = jnp.float32, jnp.bfloat16


def dft_table(width):
    index = np.arange(width)
    phase = (index[:, None] * index[None, :] % width) * (2.0 * np.pi / width)
    scale = 1.0 / np.sqrt(width)
    table = np.concatenate([np.cos(phase) * scale, -np.sin(phase) * scale], axis=1)
    return jnp.asarray(table.astype(np.float32)).astype(BF16)


def dot(a, b):
    return jnp.dot(a, b, preferred_element_type=F32)


def quad(a, b, c, d):
    return jnp.concatenate(
        [jnp.concatenate([a, b], axis=1), jnp.concatenate([c, d], axis=1)], axis=0
    )


def swap(x):
    w = x.shape[0] // 2
    return quad(x[:w, :w], x[w:, :w], x[:w, w:], x[w:, w:])


def near_first(n):
    return sorted(range(1, n), key=lambda d: min(d, n - d))


def kernel(
    n_angle,
    n_tile,
    n_cuts,
    pos_ref,
    obj_hbm,
    amp_hbm,
    probe_hbm,
    table_hbm,
    proj_hbm,
    new_ref,
    vol_ref,
    obj,
    amp,
    probe,
    table,
    proj,
    bands,
    image,
    fwd,
    bwd,
    terms,
    canvas,
    first_x,
    first_y,
    slab_sum,
    staged,
    last_x,
    last_y,
    real_first,
    real_sum,
    real_staged,
    real_last,
    phase,
    load_sem,
    send_sem,
    recv_sem,
):
    a, t, c = lax.axis_index("angle"), lax.axis_index("tile"), lax.axis_index("cuts")
    z, core = a // CORES, lax.rem(a, CORES)
    n_z = n_angle // CORES
    rows, pixels = obj.shape[1:]
    width = probe.shape[-1]
    strips = pixels // LANES
    half = pixels // 2
    n_patch = amp.shape[0]
    pad = pixels - width
    x_steps, y_steps, z_steps = near_first(n_tile), near_first(n_cuts), near_first(n_z)

    def ahead(at, step, n):
        return lax.rem(at + step, n)

    def behind(at, step, n):
        return lax.rem(at + n - step, n)

    def x_peer(d):
        return {"tile": ahead(t, d, n_tile)}

    def y_peer(d):
        return {"cuts": ahead(c, d, n_cuts)}

    def z_peer(d):
        return {"angle": ahead(z, d, n_z) * CORES + core}

    sibling = {"angle": z * CORES + (1 - core)}
    sent = []

    def remote(src, dst, device):
        i = len(sent)
        copy = pltpu.make_async_remote_copy(
            src_ref=src,
            dst_ref=dst,
            send_sem=send_sem.at[i],
            recv_sem=recv_sem.at[i],
            device_id=device,
            device_id_type=MESH,
        )
        copy.start()
        sent.append(copy)
        return copy

    loads = [
        pltpu.make_async_copy(src, dst, load_sem.at[i])
        for i, (src, dst) in enumerate(
            [
                (obj_hbm, obj),
                (probe_hbm, probe),
                (table_hbm, table),
                (amp_hbm, amp),
                (proj_hbm, proj),
            ]
        )
    ]
    for load in loads:
        load.start()
    barrier = pltpu.get_barrier_semaphore()
    greeted = [x_peer(d) for d in x_steps] + [y_peer(d) for d in y_steps]
    greeted += [z_peer(d) for d in z_steps] + [sibling]
    for device in greeted:
        pl.semaphore_signal(barrier, inc=1, device_id=device, device_id_type=MESH)
    loads[0].wait()
    for part in range(2):
        bands[part, t, c] = obj[part].astype(BF16)
    pl.semaphore_wait(barrier, len(greeted))

    first, second = {}, {}

    def go_x(part, tt, cc, key):
        for d in x_steps:
            block = bands.at[part, tt, cc]
            key[d] = remote(block, block, x_peer(d))

    def go_y(part, tt, cc, key):
        for d in y_steps:
            block = bands.at[part, tt, cc]
            key[d] = remote(block, block, y_peer(d))

    for part in range(2):
        first[part] = {}
        second[part, 0] = {}
    go_x(0, t, c, first[0])
    go_y(1, t, c, first[1])
    go_y(0, t, c, second[0, 0])
    go_x(1, t, c, second[1, 0])

    terms_zero = jnp.zeros((pad, LANES), F32)

    @pl.loop(0, n_patch)
    def _(p):
        for part in range(2):
            terms[p, part, :pad] = terms_zero
            terms[p, part, pad + width :] = terms_zero

    loads[1].wait()
    loads[2].wait()
    f_re, f_im = table[:, :width], table[:, width:]
    fwd[...] = quad(f_re, f_im, -f_im, f_re)
    bwd[...] = quad(f_re, -f_im, f_im, f_re)

    def unpack(part, tt, cc):
        at = pl.ds(pl.multiple_of((tt * n_cuts + cc) * rows, rows), rows)
        block = bands[part, tt, cc]
        for j in range(strips):
            image[part, j, at, :] = block[:, j * LANES : (j + 1) * LANES].astype(F32)

    unpack(0, t, c)
    unpack(1, t, c)
    for i in range(max(len(x_steps), len(y_steps))):
        if i < len(x_steps):
            d = x_steps[i]
            first[0][d].wait_recv()
            second[0, d] = {}
            go_y(0, behind(t, d, n_tile), c, second[0, d])
        if i < len(y_steps):
            d = y_steps[i]
            first[1][d].wait_recv()
            second[1, d] = {}
            go_x(1, t, behind(c, d, n_cuts), second[1, d])
    for d in x_steps:
        unpack(0, behind(t, d, n_tile), c)
    for d in y_steps:
        unpack(1, t, behind(c, d, n_cuts))
    for d in [0] + x_steps:
        for e in y_steps:
            second[0, d][e].wait_recv()
            unpack(0, behind(t, d, n_tile), behind(c, e, n_cuts))
    for d in [0] + y_steps:
        for e in x_steps:
            second[1, d][e].wait_recv()
            unpack(1, behind(t, e, n_tile), behind(c, d, n_cuts))
    loads[3].wait()

    lane = lax.broadcasted_iota(jnp.int32, (width, LANES), 1)

    def pair(i, carry):
        exits = []
        p_re, p_im = probe[0], probe[1]
        for k in range(2):
            row, col = pos_ref[0, 2 * i + k], pos_ref[1, 2 * i + k]
            strip, shift = col // LANES, lax.rem(col, LANES)

            def window(part):
                left = image[part, strip, pl.ds(row, width), :]
                right = image[part, jnp.minimum(strip + 1, strips - 1), pl.ds(row, width), :]
                joined = jnp.where(lane >= shift, left, right)
                return pltpu.roll(joined, lax.rem(LANES - shift, LANES), 1)

            w_re, w_im = window(0), window(1)
            exits.append((p_re * w_re - p_im * w_im, p_re * w_im + p_im * w_re))
        spread = dot(quad(*exits[0], *exits[1]).astype(BF16), fwd[...]).astype(BF16)
        spectrum = dot(bwd[...], swap(spread))
        s_re, s_im = spectrum[:width], spectrum[width:]
        measured = jnp.concatenate([amp[2 * i], amp[2 * i + 1]], axis=1).astype(F32)
        scaling = measured * lax.rsqrt(jnp.maximum(s_re * s_re + s_im * s_im, 1.0))
        projected = jnp.concatenate([s_re * scaling, s_im * scaling], axis=0).astype(BF16)
        back = dot(swap(projected), bwd[...]).astype(BF16)
        revised = dot(fwd[...], swap(back))
        for k in range(2):
            shift = lax.rem(pos_ref[1, 2 * i + k], LANES)
            cols = slice(k * width, (k + 1) * width)
            d_re = revised[:width, cols] - exits[k][0]
            d_im = revised[width:, cols] - exits[k][1]
            u_re = STEP_SIZE * (p_re * d_re + p_im * d_im)
            u_im = STEP_SIZE * (p_re * d_im - p_im * d_re)
            terms[2 * i + k, 0, pad : pad + width] = pltpu.roll(u_re, shift, 1)
            terms[2 * i + k, 1, pad : pad + width] = pltpu.roll(u_im, shift, 1)
        return carry

    lax.fori_loop(0, n_patch // 2, pair, 0)

    piece = 64
    lane8 = lax.broadcasted_iota(jnp.int32, (8, LANES), 1)

    def build(part, slab):
        for q in range(n_cuts * rows // piece):
            base = pad + slab * (n_cuts * rows) + q * piece

            def add(p, totals):
                row, col = pos_ref[0, p], pos_ref[1, p]
                strip, shift = col // LANES, lax.rem(col, LANES)
                block = terms[p, part, pl.ds(base - row, piece), :].reshape(piece // 8, 8, LANES)
                place = strip + jnp.where(lane8 < shift, 1, 0)
                return tuple(
                    total + jnp.where((place == j)[None], block, 0.0)
                    for j, total in enumerate(totals)
                )

            zero = jnp.zeros((piece // 8, 8, LANES), F32)
            totals = lax.fori_loop(0, n_patch, add, (zero,) * strips, unroll=2)
            for h in range(2):
                wide = jnp.concatenate(
                    [x.reshape(piece, LANES) for x in totals[h * strips // 2 : (h + 1) * strips // 2]],
                    axis=1,
                ).astype(BF16)
                for b in range(piece // rows):
                    canvas[part, h, slab, q * (piece // rows) + b] = wide[b * rows : (b + 1) * rows]

    sum_x, sum_y = {}, {}
    for d in reversed(x_steps):
        slab = ahead(t, d, n_tile)
        build(1, slab)
        sum_x[d] = remote(canvas.at[1, 0, slab], first_x.at[d - 1], x_peer(d))
    build(1, t)
    for d in reversed(y_steps):
        sum_y[d] = remote(canvas.at[1, 1, :, ahead(c, d, n_cuts)], first_y.at[d - 1], y_peer(d))
    for d in reversed(x_steps):
        build(0, ahead(t, d, n_tile))
    build(0, t)

    fin_x, fin_y = {}, {}
    for d in x_steps:
        sum_x[d].wait_recv()
    total = canvas[1, 0, t].astype(F32)
    for d in x_steps:
        total = total + first_x[d - 1].astype(F32)
    slab_sum[0] = total
    staged[0] = total.astype(BF16)
    for d in reversed(y_steps):
        fin_y[d] = remote(staged.at[0, ahead(c, d, n_cuts)], last_y.at[d - 1], y_peer(d))
    for d in y_steps:
        sum_y[d].wait_recv()
    for tt in range(n_tile):
        total = canvas[1, 1, tt, c].astype(F32)
        for d in y_steps:
            total = total + first_y[d - 1, tt].astype(F32)
        slab_sum[1, tt] = total
        staged[1, tt] = total.astype(BF16)
    for d in reversed(x_steps):
        fin_x[d] = remote(staged.at[1, ahead(t, d, n_tile)], last_x.at[d - 1], x_peer(d))
    for d in y_steps:
        fin_y[d].wait_recv()
    left = slab_sum[0, c]
    for d in y_steps:
        left = left + last_y[d - 1].astype(F32)
    for d in x_steps:
        fin_x[d].wait_recv()
    right = slab_sum[1, t]
    for d in x_steps:
        right = right + last_x[d - 1].astype(F32)
    update = jnp.concatenate([left, right], axis=1)
    phase[a, c] = (bands[1, t, c].astype(F32) + update).astype(BF16)
    new_ref[1] = obj[1] + update

    z_copies, y_copies, s_copies = {}, {}, {}

    def block_at(dz, dc):
        return phase.at[behind(z, dz, n_z) * CORES + core, behind(c, dc, n_cuts)]

    def to_sibling(dz, dc):
        block = block_at(dz, dc)
        s_copies[dz, dc] = remote(block, block, sibling)

    def to_cuts(dz):
        block = block_at(dz, 0)
        for dc in y_steps:
            y_copies[dz, dc] = remote(block, block, y_peer(dc))

    own = block_at(0, 0)
    for dz in z_steps:
        z_copies[dz] = remote(own, own, z_peer(dz))
    to_cuts(0)
    to_sibling(0, 0)

    real_x, real_y = {}, {}
    for d in reversed(x_steps):
        real_x[d] = remote(canvas.at[0, :, ahead(t, d, n_tile)], real_first.at[d - 1], x_peer(d))

    for dz in z_steps:
        z_copies[dz].wait_recv()
        to_cuts(dz)
        to_sibling(dz, 0)

    for d in x_steps:
        real_x[d].wait_recv()
    for h in range(2):
        total = canvas[0, h, t].astype(F32)
        for d in x_steps:
            total = total + real_first[d - 1, h].astype(F32)
        real_sum[h] = total
        for cc in range(n_cuts):
            real_staged[cc, h] = total[cc].astype(BF16)
    for d in y_steps:
        real_y[d] = remote(real_staged.at[ahead(c, d, n_cuts)], real_last.at[d - 1], y_peer(d))

    loads[4].wait()

    def project(angle, start):
        block = phase[angle].reshape(n_cuts * rows, pixels)
        weights = proj[pl.ds(pl.multiple_of(angle * pixels, pixels), pixels), :]
        term = dot(block, weights)
        if start:
            vol_ref[...] = term
        else:
            vol_ref[...] += term

    order = [0] + z_steps
    for dz in order:
        for dc in y_steps:
            y_copies[dz, dc].wait_recv()
            to_sibling(dz, dc)
        project(behind(z, dz, n_z) * CORES + core, dz == 0)
    for d in y_steps:
        real_y[d].wait_recv()
    for h in range(2):
        total = real_sum[h, c]
        for d in y_steps:
            total = total + real_last[d - 1, h].astype(F32)
        cols = slice(h * half, (h + 1) * half)
        new_ref[0, :, cols] = obj[0, :, cols] + total
    for dz in order:
        for dc in [0] + y_steps:
            s_copies[dz, dc].wait_recv()
        project(behind(z, dz, n_z) * CORES + (1 - core), False)
    for copy in sent:
        copy.wait_send()


def body(objects, illumination, positions, amplitudes, projector):
    n_angle, n_tile, n_cuts = (lax.axis_size(n) for n in ("angle", "tile", "cuts"))
    _, _, rows, pixels = objects.shape
    n_patch = positions.shape[1]
    width = illumination.shape[-1]
    strips = pixels // LANES
    half = pixels // 2
    pad = pixels - width
    vmem = pl.BlockSpec(memory_space=pltpu.VMEM)
    hbm = pl.BlockSpec(memory_space=pltpu.HBM)

    new_objects, volume = pl.pallas_call(
        functools.partial(kernel, n_angle, n_tile, n_cuts),
        out_shape=(
            jax.ShapeDtypeStruct((2, rows, pixels), F32),
            jax.ShapeDtypeStruct((n_cuts * rows, projector.shape[1]), F32),
        ),
        in_specs=[pl.BlockSpec(memory_space=pltpu.SMEM)] + [hbm] * 5,
        out_specs=(vmem, vmem),
        scratch_shapes=[
            pltpu.VMEM((2, rows, pixels), F32),
            pltpu.VMEM((n_patch, width, width), BF16),
            pltpu.VMEM((2, width, width), F32),
            pltpu.VMEM((width, 2 * width), BF16),
            pltpu.VMEM(projector.shape, BF16),
            pltpu.VMEM((2, n_tile, n_cuts, rows, pixels), BF16),
            pltpu.VMEM((2, strips, pixels, LANES), F32),
            pltpu.VMEM((2 * width, 2 * width), BF16),
            pltpu.VMEM((2 * width, 2 * width), BF16),
            pltpu.VMEM((n_patch, 2, 2 * pad + width, LANES), F32),
            pltpu.VMEM((2, 2, n_tile, n_cuts, rows, half), BF16),
            pltpu.VMEM((n_tile - 1, n_cuts, rows, half), BF16),
            pltpu.VMEM((n_cuts - 1, n_tile, rows, half), BF16),
            pltpu.VMEM((2, n_cuts, rows, half), F32),
            pltpu.VMEM((2, n_cuts, rows, half), BF16),
            pltpu.VMEM((n_tile - 1, rows, half), BF16),
            pltpu.VMEM((n_cuts - 1, rows, half), BF16),
            pltpu.VMEM((n_tile - 1, 2, n_cuts, rows, half), BF16),
            pltpu.VMEM((2, n_cuts, rows, half), F32),
            pltpu.VMEM((n_cuts, 2, rows, half), BF16),
            pltpu.VMEM((n_cuts - 1, 2, rows, half), BF16),
            pltpu.VMEM((n_angle, n_cuts, rows, pixels), BF16),
            pltpu.SemaphoreType.DMA((5,)),
            pltpu.SemaphoreType.DMA((COPIES,)),
            pltpu.SemaphoreType.DMA((COPIES,)),
        ],
        compiler_params=pltpu.CompilerParams(
            collective_id=0, has_side_effects=True, vmem_limit_bytes=56 * 2**20
        ),
        name="update_and_project",
    )(positions[0].T, objects[0], amplitudes[0], illumination, dft_table(width), projector)
    return new_objects[None], volume


def solution(mesh):
    in_specs = (
        P("angle", None, ("tile", "cuts"), None),
        P(),
        P("angle", ("tile", "cuts"), None),
        P("angle", ("tile", "cuts"), None, None),
        P(None, ("angle", "cuts")),
    )
    out_specs = (P("angle", None, ("tile", "cuts"), None), P("tile", ("angle", "cuts")))
    return jax.shard_map(body, mesh=mesh, in_specs=in_specs, out_specs=out_specs, check_vma=False)
```

time: 395 us -> 61.2 us (0.15)
  waiting for transfers between devices: 186 us -> 0 us
  local copies, waits for them, and re-layouts: 99.6 us -> 3.24 us
  loops' own time: 57.9 us -> 0 us
  Pallas kernels: 0 us -> 57.1 us
  other arithmetic: 26.2 us -> 0 us
  between operations: 14 us -> 0.64 us
  matrix products: 8.83 us -> 0 us
    psum x1 -> x0, waiting for transfers between devices: 96.9 us -> none  [body(): lax.psum(partial_value.astype(jnp.bfloat16), ('tile', 'cuts'))]
    all_gather x2 -> x0, waiting for transfers between devices: 89.4 us -> none  [the longest x1 49.1 us: body(): lax.all_gather(object_half, ('tile', 'cuts'), axis=2, tiled=True)]
    another operation x2 -> x0, loops' own time: 57.9 us -> none  [the longest x1 57.7 us: patch_update(): return lax.fori_loop(0, place_list.shape[0], place_one, canvas)]
    pallas_call x0 -> x1, Pallas kernels: none -> 57.1 us  [body(): pl.pallas_call(functools.partial(kernel, n_angle, n_tile, n_cuts), out_sh...]
    gather x48 -> x0, local copies, waits for them, and re-layouts: 45.8 us -> none
    dynamic_update_slice x16 -> x0, local copies, waits for them, and re-layouts: 38.4 us -> none  [place_one(): lax.dynamic_update_slice(canvas_now, current + patch_terms[counter], (zer...]
    add x17 -> x0, other arithmetic: 17 us -> none  [the longest x16 16.4 us: place_one(): current + patch_terms[counter]]
    dynamic_slice x16 -> x0, local copies, waits for them, and re-layouts: 9.38 us -> none  [place_one(): col_at = place_list[counter, 1]]
  transfers between devices with their start and end apart: 3 -> 0, of which waited for: 3 -> 0; matrix products, arithmetic and copies ran while one was open for 1% -> 0% of each run, Pallas kernels for 0% -> 0%
where the time goes in v2:
time: 61.2 us; the launch traced here: 61 us
  Pallas kernels  57.1 us (93%)
  local copies, waits for them, and re-layouts  3.24 us (5%)
  between operations  0.64 us (1%)
    pallas_call x1, Pallas kernels, body(): pl.pallas_call(functools.partial(kernel, n_angle, n_tile, n_cuts), out_sh...  57.1 us
    unnamed x2, local copies, waits for them, and re-layouts  3.24 us

profile of v2, /device:TPU:1, one launch (start us, length us, event | category | flops | bytes accessed | tf_op | source)
XLA Modules:
  0.0 61.0 jit_solution(625267741465022875)
XLA Ops:
  0.6 57.1 %update_and_project.1 = (f32[2,32,512]{2,1,0:T(8,128)}, f32[128,512]{1,0:T(8,128)}) custom-call(s32[2,16]{1,0:T(2,128)} %bitcast.9, f32[2,32,512]{2,1,0:T(8,128)} %bitcast.7, bf16[16,128,128]{2,1,0:T(8,128)(2,1)} %bitcast.6, f32[2,128,128]{2,1,0:T(8,128)} %probe_hbm.1, bf16[128,256]{1,0:T(8,128)(2,1)} %constant.6.table_hbm, bf16[8192,512]{1,0:T(8,128)(2,1)} %proj_hbm.1), custom_call_target="tpu_custom_call" | custom-call | tf_op jit(solution)/shard_map/update_and_project/pallas_call | solution.py:414
  57.8 1.6 %copy.10 = f32[1,2,32,512]{3,2,1,0:T(8,128)} copy(f32[1,2,32,512]{3,2,1,0:T(8,128)} %bitcast.8) | data formatting | bytes 262144
  59.3 1.7 %copy.11 = f32[128,512]{1,0:T(8,128)} copy(f32[128,512]{1,0:T(8,128)} %get-tuple-element.9) | data formatting | bytes 524288

commit v3 on v2

--- a/solution.py
+++ b/solution.py
@@ -47,7 +47,7 @@
     n_angle,
     n_tile,
     n_cuts,
-    pos_ref,
+    pos_hbm,
     obj_hbm,
     amp_hbm,
     probe_hbm,
@@ -77,6 +77,7 @@
     real_staged,
     real_last,
     phase,
+    pos_ref,
     load_sem,
     send_sem,
     recv_sem,
@@ -129,6 +130,7 @@
         for i, (src, dst) in enumerate(
             [
                 (obj_hbm, obj),
+                (pos_hbm, pos_ref),
                 (probe_hbm, probe),
                 (table_hbm, table),
                 (amp_hbm, amp),
@@ -136,7 +138,7 @@
             ]
         )
     ]
-    for load in loads:
+    for load in loads[:5]:
         load.start()
     barrier = pltpu.get_barrier_semaphore()
     greeted = [x_peer(d) for d in x_steps] + [y_peer(d) for d in y_steps]
@@ -167,6 +169,7 @@
     go_y(1, t, c, first[1])
     go_y(0, t, c, second[0, 0])
     go_x(1, t, c, second[1, 0])
+    loads[5].start()
 
     terms_zero = jnp.zeros((pad, LANES), F32)
 
@@ -176,8 +179,8 @@
             terms[p, part, :pad] = terms_zero
             terms[p, part, pad + width :] = terms_zero
 
-    loads[1].wait()
     loads[2].wait()
+    loads[3].wait()
     f_re, f_im = table[:, :width], table[:, width:]
     fwd[...] = quad(f_re, f_im, -f_im, f_re)
     bwd[...] = quad(f_re, -f_im, f_im, f_re)
@@ -213,7 +216,8 @@
         for e in x_steps:
             second[1, d][e].wait_recv()
             unpack(1, behind(t, e, n_tile), behind(c, d, n_cuts))
-    loads[3].wait()
+    loads[4].wait()
+    loads[1].wait()
 
     lane = lax.broadcasted_iota(jnp.int32, (width, LANES), 1)
 
@@ -251,7 +255,7 @@
             terms[2 * i + k, 1, pad : pad + width] = pltpu.roll(u_im, shift, 1)
         return carry
 
-    lax.fori_loop(0, n_patch // 2, pair, 0)
+    lax.fori_loop(0, n_patch // 2, pair, 0, unroll=True)
 
     piece = 64
     lane8 = lax.broadcasted_iota(jnp.int32, (8, LANES), 1)
@@ -271,7 +275,7 @@
                 )
 
             zero = jnp.zeros((piece // 8, 8, LANES), F32)
-            totals = lax.fori_loop(0, n_patch, add, (zero,) * strips, unroll=2)
+            totals = lax.fori_loop(0, n_patch, add, (zero,) * strips, unroll=True)
             for h in range(2):
                 wide = jnp.concatenate(
                     [x.reshape(piece, LANES) for x in totals[h * strips // 2 : (h + 1) * strips // 2]],
@@ -326,48 +330,53 @@
     phase[a, c] = (bands[1, t, c].astype(F32) + update).astype(BF16)
     new_ref[1] = obj[1] + update
 
-    z_copies, y_copies, s_copies = {}, {}, {}
+    z_copies, y_copies, far_copies, s_copies = {}, {}, {}, {}
+    order = [0] + z_steps
+    opposite = n_cuts // 2
+    near = [1, n_cuts - 1]
+    close = z_steps[:4]
+
+    def angle_of(dz, which):
+        return behind(z, dz, n_z) * CORES + which
 
     def block_at(dz, dc):
-        return phase.at[behind(z, dz, n_z) * CORES + core, behind(c, dc, n_cuts)]
-
-    def to_sibling(dz, dc):
-        block = block_at(dz, dc)
-        s_copies[dz, dc] = remote(block, block, sibling)
-
-    def to_cuts(dz):
-        block = block_at(dz, 0)
-        for dc in y_steps:
-            y_copies[dz, dc] = remote(block, block, y_peer(dc))
+        return phase.at[angle_of(dz, core), behind(c, dc, n_cuts)]
 
     own = block_at(0, 0)
+    y_copies[0, opposite] = remote(own, own, y_peer(opposite))
     for dz in z_steps:
         z_copies[dz] = remote(own, own, z_peer(dz))
-    to_cuts(0)
-    to_sibling(0, 0)
 
     real_x, real_y = {}, {}
-    for d in reversed(x_steps):
-        real_x[d] = remote(canvas.at[0, :, ahead(t, d, n_tile)], real_first.at[d - 1], x_peer(d))
-
-    for dz in z_steps:
-        z_copies[dz].wait_recv()
-        to_cuts(dz)
-        to_sibling(dz, 0)
-
-    for d in x_steps:
-        real_x[d].wait_recv()
-    for h in range(2):
-        total = canvas[0, h, t].astype(F32)
+
+    def real_begin():
+        for d in reversed(x_steps):
+            real_x[d] = remote(
+                canvas.at[0, :, ahead(t, d, n_tile)], real_first.at[d - 1], x_peer(d)
+            )
+
+    def real_middle():
         for d in x_steps:
-            total = total + real_first[d - 1, h].astype(F32)
-        real_sum[h] = total
-        for cc in range(n_cuts):
-            real_staged[cc, h] = total[cc].astype(BF16)
-    for d in y_steps:
-        real_y[d] = remote(real_staged.at[ahead(c, d, n_cuts)], real_last.at[d - 1], y_peer(d))
-
-    loads[4].wait()
+            real_x[d].wait_recv()
+        for h in range(2):
+            total = canvas[0, h, t].astype(F32)
+            for d in x_steps:
+                total = total + real_first[d - 1, h].astype(F32)
+            real_sum[h] = total
+            for cc in range(n_cuts):
+                real_staged[cc, h] = total[cc].astype(BF16)
+        for d in y_steps:
+            real_y[d] = remote(real_staged.at[ahead(c, d, n_cuts)], real_last.at[d - 1], y_peer(d))
+
+    def real_end():
+        for d in y_steps:
+            real_y[d].wait_recv()
+        for h in range(2):
+            total = real_sum[h, c]
+            for d in y_steps:
+                total = total + real_last[d - 1, h].astype(F32)
+            cols = slice(h * half, (h + 1) * half)
+            new_ref[0, :, cols] = obj[0, :, cols] + total
 
     def project(angle, start):
         block = phase[angle].reshape(n_cuts * rows, pixels)
@@ -378,26 +387,61 @@
         else:
             vol_ref[...] += term
 
-    order = [0] + z_steps
+    def to_sibling(dz, dc):
+        block = block_at(dz, dc)
+        s_copies[dz, dc] = remote(block, block, sibling)
+
+    for dc in near:
+        y_copies[0, dc] = remote(own, own, y_peer(dc))
+    to_sibling(0, 0)
+    real_begin()
+    y_copies[0, opposite].wait_recv()
+    to_sibling(0, opposite)
+    block = block_at(0, opposite)
+    for dz in close:
+        far_copies[dz] = remote(block, block, z_peer(dz))
+    for dz in z_steps:
+        z_copies[dz].wait_recv()
+        block = block_at(dz, 0)
+        for dc in near if dz in close else [opposite] + near:
+            y_copies[dz, dc] = remote(block, block, y_peer(dc))
+        to_sibling(dz, 0)
+    real_middle()
+    loads[5].wait()
     for dz in order:
-        for dc in y_steps:
-            y_copies[dz, dc].wait_recv()
-            to_sibling(dz, dc)
-        project(behind(z, dz, n_z) * CORES + core, dz == 0)
-    for d in y_steps:
-        real_y[d].wait_recv()
-    for h in range(2):
-        total = real_sum[h, c]
-        for d in y_steps:
-            total = total + real_last[d - 1, h].astype(F32)
-        cols = slice(h * half, (h + 1) * half)
-        new_ref[0, :, cols] = obj[0, :, cols] + total
+        for dc in near + [opposite]:
+            if dc == opposite and dz in close:
+                far_copies[dz].wait_recv()
+            elif (dz, dc) != (0, opposite):
+                y_copies[dz, dc].wait_recv()
+            if (dz, dc) != (0, opposite):
+                to_sibling(dz, dc)
+        project(angle_of(dz, core), dz == 0)
+    real_end()
     for dz in order:
-        for dc in [0] + y_steps:
+        for dc in range(n_cuts):
             s_copies[dz, dc].wait_recv()
-        project(behind(z, dz, n_z) * CORES + (1 - core), False)
+        project(angle_of(dz, 1 - core), False)
     for copy in sent:
         copy.wait_send()
+
+
+def hand_on(new_src, vol_src, new_ref, vol_ref, new_held, vol_held, sem):
+    way_in = [
+        pltpu.make_async_copy(new_src, new_held, sem.at[0]),
+        pltpu.make_async_copy(vol_src, vol_held, sem.at[1]),
+    ]
+    way_out = [
+        pltpu.make_async_copy(new_held, new_ref, sem.at[2]),
+        pltpu.make_async_copy(vol_held, vol_ref, sem.at[3]),
+    ]
+    for copy in way_in:
+        copy.start()
+    for copy, onward in zip(way_in, way_out):
+        copy.wait()
+        onward.start()
+    for copy in way_out:
+        copy.wait()
 
 
 def body(objects, illumination, positions, amplitudes, projector):
@@ -417,7 +461,7 @@
             jax.ShapeDtypeStruct((2, rows, pixels), F32),
             jax.ShapeDtypeStruct((n_cuts * rows, projector.shape[1]), F32),
         ),
-        in_specs=[pl.BlockSpec(memory_space=pltpu.SMEM)] + [hbm] * 5,
+        in_specs=[hbm] * 6,
         out_specs=(vmem, vmem),
         scratch_shapes=[
             pltpu.VMEM((2, rows, pixels), F32),
@@ -442,7 +486,8 @@
             pltpu.VMEM((n_cuts, 2, rows, half), BF16),
             pltpu.VMEM((n_cuts - 1, 2, rows, half), BF16),
             pltpu.VMEM((n_angle, n_cuts, rows, pixels), BF16),
-            pltpu.SemaphoreType.DMA((5,)),
+            pltpu.SMEM((2, n_patch), jnp.int32),
+            pltpu.SemaphoreType.DMA((6,)),
             pltpu.SemaphoreType.DMA((COPIES,)),
             pltpu.SemaphoreType.DMA((COPIES,)),
         ],
@@ -451,6 +496,22 @@
         ),
         name="update_and_project",
     )(positions[0].T, objects[0], amplitudes[0], illumination, dft_table(width), projector)
+    any_place = pl.BlockSpec(memory_space=pl.ANY)
+    new_objects, volume = pl.pallas_call(
+        hand_on,
+        out_shape=(
+            jax.ShapeDtypeStruct(new_objects.shape, F32),
+            jax.ShapeDtypeStruct(volume.shape, F32),
+        ),
+        in_specs=[any_place] * 2,
+        out_specs=(any_place, any_place),
+        scratch_shapes=[
+            pltpu.VMEM(new_objects.shape, F32),
+            pltpu.VMEM(volume.shape, F32),
+            pltpu.SemaphoreType.DMA((4,)),
+        ],
+        name="hand_on",
+    )(new_objects, volume)
     return new_objects[None], volume
 
 

time: 61.2 us -> 53.9 us (0.88)
  Pallas kernels: 57.1 us -> 53.2 us
  local copies, waits for them, and re-layouts: 3.24 us -> 0 us
    pallas_call x1, Pallas kernels: 57.1 us -> 51.4 us  [body(): pl.pallas_call(functools.partial(kernel, n_angle, n_tile, n_cuts), out_sh...]
    unnamed x2 -> x0, local copies, waits for them, and re-layouts: 3.24 us -> none
    pallas_call x0 -> x1, Pallas kernels: none -> 1.76 us  [body(): pl.pallas_call(hand_on, out_shape=(jax.ShapeDtypeStruct(new_objects.shape...]
where the time goes in v3:
time: 53.9 us; the launch traced here: 53.8 us
  Pallas kernels  53.2 us (99%)
  between operations  0.64 us (1%)
    pallas_call x1, Pallas kernels, body(): pl.pallas_call(functools.partial(kernel, n_angle, n_tile, n_cuts), out_sh...  51.4 us
    pallas_call x1, Pallas kernels, body(): pl.pallas_call(hand_on, out_shape=(jax.ShapeDtypeStruct(new_objects.shape...  1.76 us

profile of v3, /device:TPU:1, one launch (start us, length us, event | category | flops | bytes accessed | tf_op | source)
XLA Modules:
  0.0 53.8 jit_solution(6281157574662051836)
XLA Ops:
  0.6 51.4 %update_and_project.1 = (f32[2,32,512]{2,1,0:T(8,128)}, f32[128,512]{1,0:T(8,128)}) custom-call(s32[2,16]{1,0:T(2,128)} %bitcast.8, f32[2,32,512]{2,1,0:T(8,128)} %bitcast.7, bf16[16,128,128]{2,1,0:T(8,128)(2,1)} %bitcast.6, f32[2,128,128]{2,1,0:T(8,128)} %probe_hbm.1, bf16[128,256]{1,0:T(8,128)(2,1)} %constant.6.table_hbm, bf16[8192,512]{1,0:T(8,128)(2,1)} %proj_hbm.1), custom_call_target="tpu_custom_call" | custom-call | tf_op jit(solution)/shard_map/update_and_project/pallas_call | solution.py:458
  52.1 1.8 %hand_on.1 = (f32[2,32,512]{2,1,0:T(8,128)}, f32[128,512]{1,0:T(8,128)}) custom-call(f32[2,32,512]{2,1,0:T(8,128)} %get-tuple-element.6.new_src, f32[128,512]{1,0:T(8,128)} %get-tuple-element.7.vol_src), custom_call_target="tpu_custom_call" | custom-call | tf_op jit(solution)/shard_map/hand_on/pallas_call | solution.py:500

commit v4 on v3

--- a/solution.py
+++ b/solution.py
@@ -426,21 +426,14 @@
         copy.wait_send()
 
 
-def hand_on(new_src, vol_src, new_ref, vol_ref, new_held, vol_held, sem):
-    way_in = [
-        pltpu.make_async_copy(new_src, new_held, sem.at[0]),
-        pltpu.make_async_copy(vol_src, vol_held, sem.at[1]),
+def hand_on(new_src, vol_src, new_ref, vol_ref, sem):
+    copies = [
+        pltpu.make_async_copy(new_src, new_ref, sem.at[0]),
+        pltpu.make_async_copy(vol_src, vol_ref, sem.at[1]),
     ]
-    way_out = [
-        pltpu.make_async_copy(new_held, new_ref, sem.at[2]),
-        pltpu.make_async_copy(vol_held, vol_ref, sem.at[3]),
-    ]
-    for copy in way_in:
+    for copy in copies:
         copy.start()
-    for copy, onward in zip(way_in, way_out):
-        copy.wait()
-        onward.start()
-    for copy in way_out:
+    for copy in copies:
         copy.wait()
 
 
@@ -455,11 +448,14 @@
     vmem = pl.BlockSpec(memory_space=pltpu.VMEM)
     hbm = pl.BlockSpec(memory_space=pltpu.HBM)
 
+    operands = (
+        positions[0].T, objects[0], amplitudes[0], illumination, dft_table(width), projector
+    )
     new_objects, volume = pl.pallas_call(
         functools.partial(kernel, n_angle, n_tile, n_cuts),
         out_shape=(
-            jax.ShapeDtypeStruct((2, rows, pixels), F32),
-            jax.ShapeDtypeStruct((n_cuts * rows, projector.shape[1]), F32),
+            pltpu.VMEM((2, rows, pixels), F32),
+            pltpu.VMEM((n_cuts * rows, projector.shape[1]), F32),
         ),
         in_specs=[hbm] * 6,
         out_specs=(vmem, vmem),
@@ -492,10 +488,10 @@
             pltpu.SemaphoreType.DMA((COPIES,)),
         ],
         compiler_params=pltpu.CompilerParams(
-            collective_id=0, has_side_effects=True, vmem_limit_bytes=56 * 2**20
+            collective_id=0, has_side_effects=True, vmem_limit_bytes=44 * 2**20
         ),
         name="update_and_project",
-    )(positions[0].T, objects[0], amplitudes[0], illumination, dft_table(width), projector)
+    )(*(pltpu.with_memory_space_constraint(x, pltpu.HBM) for x in operands))
     any_place = pl.BlockSpec(memory_space=pl.ANY)
     new_objects, volume = pl.pallas_call(
         hand_on,
@@ -503,15 +499,13 @@
             jax.ShapeDtypeStruct(new_objects.shape, F32),
             jax.ShapeDtypeStruct(volume.shape, F32),
         ),
-        in_specs=[any_place] * 2,
+        in_specs=[vmem] * 2,
         out_specs=(any_place, any_place),
         scratch_shapes=[
-            pltpu.VMEM(new_objects.shape, F32),
-            pltpu.VMEM(volume.shape, F32),
-            pltpu.SemaphoreType.DMA((4,)),
+            pltpu.SemaphoreType.DMA((2,)),
         ],
         name="hand_on",
-    )(new_objects, volume)
+    )(*(pltpu.with_memory_space_constraint(x, pltpu.VMEM) for x in (new_objects, volume)))
     return new_objects[None], volume
 
 

time: 53.9 us -> 52.2 us (0.968)
  Pallas kernels: 53.2 us -> 51.5 us
    pallas_call x1, Pallas kernels: 1.76 us -> 0.77 us  [body(): pl.pallas_call(hand_on, out_shape=(jax.ShapeDtypeStruct(new_objects.shape...]
    pallas_call x1, Pallas kernels: 51.4 us -> 50.7 us  [body(): pl.pallas_call(functools.partial(kernel, n_angle, n_tile, n_cuts), out_sh...]
where the time goes in v4:
time: 52.2 us; the launch traced here: 52.1 us
  Pallas kernels  51.5 us (99%)
  between operations  0.64 us (1%)
    pallas_call x1, Pallas kernels, body(): pl.pallas_call(functools.partial(kernel, n_angle, n_tile, n_cuts), out_sh...  50.7 us

profile of v4, /device:TPU:1, one launch (start us, length us, event | category | flops | bytes accessed | tf_op | source)
XLA Modules:
  0.0 52.1 jit_solution(6074805540310708123)
XLA Ops:
  0.6 50.7 %update_and_project.1 = (f32[2,32,512]{2,1,0:T(8,128)S(1)}, f32[128,512]{1,0:T(8,128)S(1)}) custom-call(s32[2,16]{1,0:T(2,128)} %bitcast.8, f32[2,32,512]{2,1,0:T(8,128)} %bitcast.7, bf16[16,128,128]{2,1,0:T(8,128)(2,1)} %bitcast.6, f32[2,128,128]{2,1,0:T(8,128)} %probe_hbm.1, bf16[128,256]{1,0:T(8,128)(2,1)} %constant.6.table_hbm, bf16[8192,512]{1,0:T(8,128)(2,1)} %proj_hbm.1), custom_call_target="tpu_custom_call" | custom-call | tf_op jit(solution)/shard_map/update_and_project/pallas_call | solution.py:454
  51.3 0.8 %hand_on.1 = (f32[2,32,512]{2,1,0:T(8,128)}, f32[128,512]{1,0:T(8,128)}) custom-call(f32[2,32,512]{2,1,0:T(8,128)S(1)} %get-tuple-element.6.new_src, f32[128,512]{1,0:T(8,128)S(1)} %get-tuple-element.7.vol_src), custom_call_target="tpu_custom_call" | custom-call | tf_op jit(solution)/shard_map/hand_on/pallas_call | solution.py:496

commit v5 on v4

--- a/solution.py
+++ b/solution.py
@@ -138,13 +138,14 @@
             ]
         )
     ]
-    for load in loads[:5]:
-        load.start()
+    loads[0].start()
     barrier = pltpu.get_barrier_semaphore()
     greeted = [x_peer(d) for d in x_steps] + [y_peer(d) for d in y_steps]
     greeted += [z_peer(d) for d in z_steps] + [sibling]
     for device in greeted:
         pl.semaphore_signal(barrier, inc=1, device_id=device, device_id_type=MESH)
+    for load in loads[1:5]:
+        load.start()
     loads[0].wait()
     for part in range(2):
         bands[part, t, c] = obj[part].astype(BF16)
@@ -152,13 +153,13 @@
 
     first, second = {}, {}
 
-    def go_x(part, tt, cc, key):
-        for d in x_steps:
+    def go_x(part, tt, cc, key, steps=x_steps):
+        for d in steps:
             block = bands.at[part, tt, cc]
             key[d] = remote(block, block, x_peer(d))
 
-    def go_y(part, tt, cc, key):
-        for d in y_steps:
+    def go_y(part, tt, cc, key, steps=y_steps):
+        for d in steps:
             block = bands.at[part, tt, cc]
             key[d] = remote(block, block, y_peer(d))
 
@@ -193,29 +194,55 @@
 
     unpack(0, t, c)
     unpack(1, t, c)
-    for i in range(max(len(x_steps), len(y_steps))):
-        if i < len(x_steps):
-            d = x_steps[i]
-            first[0][d].wait_recv()
-            second[0, d] = {}
-            go_y(0, behind(t, d, n_tile), c, second[0, d])
-        if i < len(y_steps):
-            d = y_steps[i]
-            first[1][d].wait_recv()
-            second[1, d] = {}
-            go_x(1, t, behind(c, d, n_cuts), second[1, d])
+    x_far, y_far = n_tile // 2, n_cuts // 2
+    x_near, y_near = [d for d in x_steps if d != x_far], [d for d in y_steps if d != y_far]
+    turned = {}
+
+    def back_x(d):
+        return behind(t, d, n_tile)
+
+    def back_y(d):
+        return behind(c, d, n_cuts)
+
+    for dx, dy in zip(x_near, y_near):
+        first[0][dx].wait_recv()
+        second[0, dx] = {}
+        go_y(0, back_x(dx), c, second[0, dx], y_near)
+        first[1][dy].wait_recv()
+        second[1, dy] = {}
+        go_x(1, t, back_y(dy), second[1, dy], x_near)
+    first[0][x_far].wait_recv()
+    second[0, x_far] = {}
+    go_y(0, back_x(x_far), c, second[0, x_far])
+    first[1][y_far].wait_recv()
+    second[1, y_far] = {}
+    go_x(1, t, back_y(y_far), second[1, y_far])
+    second[0, 0][y_far].wait_recv()
+    turned[0] = {}
+    go_x(0, t, back_y(y_far), turned[0], x_near)
+    second[1, 0][x_far].wait_recv()
+    turned[1] = {}
+    go_y(1, back_x(x_far), c, turned[1], y_near)
     for d in x_steps:
-        unpack(0, behind(t, d, n_tile), c)
+        unpack(0, back_x(d), c)
     for d in y_steps:
-        unpack(1, t, behind(c, d, n_cuts))
-    for d in [0] + x_steps:
-        for e in y_steps:
+        unpack(1, t, back_y(d))
+    unpack(0, t, back_y(y_far))
+    unpack(1, back_x(x_far), c)
+    for d in [0] + x_near + [x_far]:
+        for e in y_near + [y_far] * (d == x_far):
             second[0, d][e].wait_recv()
-            unpack(0, behind(t, d, n_tile), behind(c, e, n_cuts))
-    for d in [0] + y_steps:
-        for e in x_steps:
+            unpack(0, back_x(d), back_y(e))
+    for d in [0] + y_near + [y_far]:
+        for e in x_near + [x_far] * (d == y_far):
             second[1, d][e].wait_recv()
-            unpack(1, behind(t, e, n_tile), behind(c, d, n_cuts))
+            unpack(1, back_x(e), back_y(d))
+    for d in x_near:
+        turned[0][d].wait_recv()
+        unpack(0, back_x(d), back_y(y_far))
+    for d in y_near:
+        turned[1][d].wait_recv()
+        unpack(1, back_x(x_far), back_y(d))
     loads[4].wait()
     loads[1].wait()
 
@@ -260,8 +287,10 @@
     piece = 64
     lane8 = lax.broadcasted_iota(jnp.int32, (8, LANES), 1)
 
-    def build(part, slab):
-        for q in range(n_cuts * rows // piece):
+    pieces = n_cuts * rows // piece
+
+    def build(part, slab, which):
+        for q in which:
             base = pad + slab * (n_cuts * rows) + q * piece
 
             def add(p, totals):
@@ -285,20 +314,29 @@
                     canvas[part, h, slab, q * (piece // rows) + b] = wide[b * rows : (b + 1) * rows]
 
     sum_x, sum_y = {}, {}
-    for d in reversed(x_steps):
-        slab = ahead(t, d, n_tile)
-        build(1, slab)
-        sum_x[d] = remote(canvas.at[1, 0, slab], first_x.at[d - 1], x_peer(d))
-    build(1, t)
-    for d in reversed(y_steps):
-        sum_y[d] = remote(canvas.at[1, 1, :, ahead(c, d, n_cuts)], first_y.at[d - 1], y_peer(d))
-    for d in reversed(x_steps):
-        build(0, ahead(t, d, n_tile))
-    build(0, t)
+    pair_size = piece // rows
+    mine, odd = c // pair_size, lax.rem(c, pair_size)
+    partner = {1: c + 1 - 2 * odd, 2: ahead(c, 2, n_cuts), 3: n_cuts - 1 - c}
+    for turn, q in enumerate((1 - mine, mine)):
+        part_rows = pl.ds(q * pair_size, pair_size)
+        for d in x_steps[::-1] + [0]:
+            slab = ahead(t, d, n_tile)
+            build(1, slab, [q])
+            if d:
+                sum_x[d, turn] = remote(
+                    canvas.at[1, 0, slab, part_rows], first_x.at[d - 1, part_rows], x_peer(d)
+                )
+        for m in (2, 3) if turn == 0 else (1,):
+            sum_y[m] = remote(
+                canvas.at[1, 1, :, partner[m]], first_y.at[m - 1], {"cuts": partner[m]}
+            )
+    for slab in range(n_tile):
+        build(0, slab, range(pieces))
 
     fin_x, fin_y = {}, {}
     for d in x_steps:
-        sum_x[d].wait_recv()
+        for turn in range(2):
+            sum_x[d, turn].wait_recv()
     total = canvas[1, 0, t].astype(F32)
     for d in x_steps:
         total = total + first_x[d - 1].astype(F32)
@@ -406,7 +444,6 @@
         for dc in near if dz in close else [opposite] + near:
             y_copies[dz, dc] = remote(block, block, y_peer(dc))
         to_sibling(dz, 0)
-    real_middle()
     loads[5].wait()
     for dz in order:
         for dc in near + [opposite]:
@@ -417,6 +454,8 @@
             if (dz, dc) != (0, opposite):
                 to_sibling(dz, dc)
         project(angle_of(dz, core), dz == 0)
+        if dz == order[3]:
+            real_middle()
     real_end()
     for dz in order:
         for dc in range(n_cuts):

time: 52.2 us -> 50.9 us (0.975)
  Pallas kernels: 51.5 us -> 50.2 us
    pallas_call x1, Pallas kernels: 50.7 us -> 49.4 us  [body(): pl.pallas_call(functools.partial(kernel, n_angle, n_tile, n_cuts), out_sh...]
where the time goes in v5:
time: 50.9 us; the launch traced here: 50.8 us
  Pallas kernels  50.2 us (99%)
  between operations  0.64 us (1%)
    pallas_call x1, Pallas kernels, body(): pl.pallas_call(functools.partial(kernel, n_angle, n_tile, n_cuts), out_sh...  49.4 us

profile of v5, /device:TPU:1, one launch (start us, length us, event | category | flops | bytes accessed | tf_op | source)
XLA Modules:
  0.0 50.8 jit_solution(11103971185318971122)
XLA Ops:
  0.6 49.4 %update_and_project.1 = (f32[2,32,512]{2,1,0:T(8,128)S(1)}, f32[128,512]{1,0:T(8,128)S(1)}) custom-call(s32[2,16]{1,0:T(2,128)} %bitcast.8, f32[2,32,512]{2,1,0:T(8,128)} %bitcast.7, bf16[16,128,128]{2,1,0:T(8,128)(2,1)} %bitcast.6, f32[2,128,128]{2,1,0:T(8,128)} %probe_hbm.1, bf16[128,256]{1,0:T(8,128)(2,1)} %constant.6.table_hbm, bf16[8192,512]{1,0:T(8,128)(2,1)} %proj_hbm.1), custom_call_target="tpu_custom_call" | custom-call | tf_op jit(solution)/shard_map/update_and_project/pallas_call | solution.py:493
  50.1 0.8 %hand_on.1 = (f32[2,32,512]{2,1,0:T(8,128)}, f32[128,512]{1,0:T(8,128)}) custom-call(f32[2,32,512]{2,1,0:T(8,128)S(1)} %get-tuple-element.6.new_src, f32[128,512]{1,0:T(8,128)S(1)} %get-tuple-element.7.vol_src), custom_call_target="tpu_custom_call" | custom-call | tf_op jit(solution)/shard_map/hand_on/pallas_call | solution.py:535

commit v6 on v5

--- a/solution.py
+++ b/solution.py
@@ -64,6 +64,9 @@
     image,
     fwd,
     bwd,
+    exits,
+    columns,
+    lines,
     terms,
     canvas,
     first_x,
@@ -248,8 +251,8 @@
 
     lane = lax.broadcasted_iota(jnp.int32, (width, LANES), 1)
 
-    def pair(i, carry):
-        exits = []
+    def spread_pair(i, carry):
+        found = []
         p_re, p_im = probe[0], probe[1]
         for k in range(2):
             row, col = pos_ref[0, 2 * i + k], pos_ref[1, 2 * i + k]
@@ -262,27 +265,42 @@
                 return pltpu.roll(joined, lax.rem(LANES - shift, LANES), 1)
 
             w_re, w_im = window(0), window(1)
-            exits.append((p_re * w_re - p_im * w_im, p_re * w_im + p_im * w_re))
-        spread = dot(quad(*exits[0], *exits[1]).astype(BF16), fwd[...]).astype(BF16)
-        spectrum = dot(bwd[...], swap(spread))
+            e_re, e_im = p_re * w_re - p_im * w_im, p_re * w_im + p_im * w_re
+            exits[2 * i + k, 0] = e_re
+            exits[2 * i + k, 1] = e_im
+            found.append((e_re, e_im))
+        columns[i] = swap(dot(quad(*found[0], *found[1]).astype(BF16), fwd[...]).astype(BF16))
+        return carry
+
+    def project_pair(i, carry):
+        spectrum = dot(bwd[...], columns[i])
         s_re, s_im = spectrum[:width], spectrum[width:]
         measured = jnp.concatenate([amp[2 * i], amp[2 * i + 1]], axis=1).astype(F32)
         scaling = measured * lax.rsqrt(jnp.maximum(s_re * s_re + s_im * s_im, 1.0))
-        projected = jnp.concatenate([s_re * scaling, s_im * scaling], axis=0).astype(BF16)
-        back = dot(swap(projected), bwd[...]).astype(BF16)
-        revised = dot(fwd[...], swap(back))
+        projected = jnp.concatenate([s_re * scaling, s_im * scaling], axis=0)
+        lines[i] = swap(projected.astype(BF16))
+        return carry
+
+    def back_pair(i, carry):
+        columns[i] = swap(dot(lines[i], bwd[...]).astype(BF16))
+        return carry
+
+    def term_pair(i, carry):
+        revised = dot(fwd[...], columns[i])
+        p_re, p_im = probe[0], probe[1]
         for k in range(2):
             shift = lax.rem(pos_ref[1, 2 * i + k], LANES)
             cols = slice(k * width, (k + 1) * width)
-            d_re = revised[:width, cols] - exits[k][0]
-            d_im = revised[width:, cols] - exits[k][1]
+            d_re = revised[:width, cols] - exits[2 * i + k, 0]
+            d_im = revised[width:, cols] - exits[2 * i + k, 1]
             u_re = STEP_SIZE * (p_re * d_re + p_im * d_im)
             u_im = STEP_SIZE * (p_re * d_im - p_im * d_re)
             terms[2 * i + k, 0, pad : pad + width] = pltpu.roll(u_re, shift, 1)
             terms[2 * i + k, 1, pad : pad + width] = pltpu.roll(u_im, shift, 1)
         return carry
 
-    lax.fori_loop(0, n_patch // 2, pair, 0, unroll=True)
+    for stage in (spread_pair, project_pair, back_pair, term_pair):
+        lax.fori_loop(0, n_patch // 2, stage, 0, unroll=True)
 
     piece = 64
     lane8 = lax.broadcasted_iota(jnp.int32, (8, LANES), 1)
@@ -508,6 +526,9 @@
             pltpu.VMEM((2, strips, pixels, LANES), F32),
             pltpu.VMEM((2 * width, 2 * width), BF16),
             pltpu.VMEM((2 * width, 2 * width), BF16),
+            pltpu.VMEM((n_patch, 2, width, width), F32),
+            pltpu.VMEM((n_patch // 2, 2 * width, 2 * width), BF16),
+            pltpu.VMEM((n_patch // 2, 2 * width, 2 * width), BF16),
             pltpu.VMEM((n_patch, 2, 2 * pad + width, LANES), F32),
             pltpu.VMEM((2, 2, n_tile, n_cuts, rows, half), BF16),
             pltpu.VMEM((n_tile - 1, n_cuts, rows, half), BF16),

time: 50.9 us -> 49.3 us (0.969)
  Pallas kernels: 50.2 us -> 48.6 us
    pallas_call x1, Pallas kernels: 49.4 us -> 47.8 us  [body(): pl.pallas_call(functools.partial(kernel, n_angle, n_tile, n_cuts), out_sh...]
where the time goes in v6:
time: 49.3 us; the launch traced here: 49.2 us
  Pallas kernels  48.6 us (99%)
  between operations  0.64 us (1%)
    pallas_call x1, Pallas kernels, body(): pl.pallas_call(functools.partial(kernel, n_angle, n_tile, n_cuts), out_sh...  47.8 us

profile of v6, /device:TPU:1, one launch (start us, length us, event | category | flops | bytes accessed | tf_op | source)
XLA Modules:
  0.0 49.2 jit_solution(6852525667170189607)
XLA Ops:
  0.6 47.8 %update_and_project.1 = (f32[2,32,512]{2,1,0:T(8,128)S(1)}, f32[128,512]{1,0:T(8,128)S(1)}) custom-call(s32[2,16]{1,0:T(2,128)} %bitcast.8, f32[2,32,512]{2,1,0:T(8,128)} %bitcast.7, bf16[16,128,128]{2,1,0:T(8,128)(2,1)} %bitcast.6, f32[2,128,128]{2,1,0:T(8,128)} %probe_hbm.1, bf16[128,256]{1,0:T(8,128)(2,1)} %constant.6.table_hbm, bf16[8192,512]{1,0:T(8,128)(2,1)} %proj_hbm.1), custom_call_target="tpu_custom_call" | custom-call | tf_op jit(solution)/shard_map/update_and_project/pallas_call | solution.py:511
  48.5 0.8 %hand_on.1 = (f32[2,32,512]{2,1,0:T(8,128)}, f32[128,512]{1,0:T(8,128)}) custom-call(f32[2,32,512]{2,1,0:T(8,128)S(1)} %get-tuple-element.6.new_src, f32[128,512]{1,0:T(8,128)S(1)} %get-tuple-element.7.vol_src), custom_call_target="tpu_custom_call" | custom-call | tf_op jit(solution)/shard_map/hand_on/pallas_call | solution.py:556

commit v7 on v6

--- a/solution.py
+++ b/solution.py
@@ -450,12 +450,12 @@
     for dc in near:
         y_copies[0, dc] = remote(own, own, y_peer(dc))
     to_sibling(0, 0)
-    real_begin()
     y_copies[0, opposite].wait_recv()
     to_sibling(0, opposite)
     block = block_at(0, opposite)
     for dz in close:
         far_copies[dz] = remote(block, block, z_peer(dz))
+    real_begin()
     for dz in z_steps:
         z_copies[dz].wait_recv()
         block = block_at(dz, 0)

time: 49.3 us -> 49.9 us (1.012); the launches traced: 49.2 us -> 49.1 us
  no operation moved by 1% of the time
where the time goes in v7:
time: 49.9 us; the launch traced here: 49.1 us
  Pallas kernels  48.5 us (97%)
  between operations  0.64 us (1%)
    pallas_call x1, Pallas kernels, body(): pl.pallas_call(functools.partial(kernel, n_angle, n_tile, n_cuts), out_sh...  47.7 us

profile of v7, /device:TPU:1, one launch (start us, length us, event | category | flops | bytes accessed | tf_op | source)
XLA Modules:
  0.0 49.1 jit_solution(11429714179346237217)
XLA Ops:
  0.6 47.7 %update_and_project.1 = (f32[2,32,512]{2,1,0:T(8,128)S(1)}, f32[128,512]{1,0:T(8,128)S(1)}) custom-call(s32[2,16]{1,0:T(2,128)} %bitcast.8, f32[2,32,512]{2,1,0:T(8,128)} %bitcast.7, bf16[16,128,128]{2,1,0:T(8,128)(2,1)} %bitcast.6, f32[2,128,128]{2,1,0:T(8,128)} %probe_hbm.1, bf16[128,256]{1,0:T(8,128)(2,1)} %constant.6.table_hbm, bf16[8192,512]{1,0:T(8,128)(2,1)} %proj_hbm.1), custom_call_target="tpu_custom_call" | custom-call | tf_op jit(solution)/shard_map/update_and_project/pallas_call | solution.py:511
  48.3 0.8 %hand_on.1 = (f32[2,32,512]{2,1,0:T(8,128)}, f32[128,512]{1,0:T(8,128)}) custom-call(f32[2,32,512]{2,1,0:T(8,128)S(1)} %get-tuple-element.6.new_src, f32[128,512]{1,0:T(8,128)S(1)} %get-tuple-element.7.vol_src), custom_call_target="tpu_custom_call" | custom-call | tf_op jit(solution)/shard_map/hand_on/pallas_call | solution.py:556
